TPU v7x, 32 devices: a whole 2x2x4 slice. The times are simulated.
32 devices in a mesh: pole: 2 (over x), row: 16 (over z, y, core).
Axes of the slice: x: 2, y: 2, z: 4, core: 2. Of those that a mesh axis runs over, the one named last changes fastest.
Arguments:
- anc_inv: bfloat16 [4096, 2048], P(('pole', 'row')), parts along dimension 0, as said below
- lower_one: bfloat16 [4096, 768], P(('pole', 'row')), parts along dimension 0, may hold values from -0.125 to 0.125
- pattern_one: int32 [16, 6], P('row'), may hold values from 0 to 1
- pivot_one: float32 [1536, 128], P('pole'), parts along dimension 0, as said below
- lower_zero: bfloat16 [4096, 512], P(('pole', 'row')), parts along dimension 0, may hold values from -0.125 to 0.125
- pattern_zero: int32 [16, 4], P('row'), may hold values from 0 to 1
- coupling_zero: bfloat16 [1536, 512], P('pole'), parts along dimension 0, may hold values from -0.21875 to 0.21875
- pattern_couple: int32 [6, 4], replicated, may hold values from 0 to 1
- pivot_zero: float32 [1024, 128], P('pole'), parts along dimension 0, as said below
Outputs:
- inv_cross: bfloat16 [4096, 768], P(('pole', 'row')), parts along dimension 0
- inv_pivot: float32 [1536, 768], P('pole'), parts along dimension 0
- inv_low: bfloat16 [4096, 512], P(('pole', 'row')), parts along dimension 0
- inv_couple: float32 [1536, 512], P('pole'), parts along dimension 0
- inv_diag: float32 [1024, 512], P('pole'), parts along dimension 0
There are 2 independent parts, one for each index of `pole`. A program takes and returns all parts, laid end to end along the dimension named above; an argument that names none is the same for every part. Nothing has to cross between parts.
Inputs may be any that keep to these rules, and one draw needn't show every extreme that they name: anc_inv equals its transpose. Each stacked block of pivot_one equals its transpose. Each stacked block of pivot_zero equals its transpose.
All inputs are finite; a program needn't handle non-finite values.
Results may differ from a plain program's by a relative error of at most 0.0037.
Values may be sent and summed in bfloat16 or wider, within the bound.
A program may use at most 128 MiB of HBM per device.

v0:
```python
import jax
import jax.numpy as jnp
from jax import lax
from jax.sharding import PartitionSpec as P


def masked(values, pattern):
    rows, cols = pattern.shape
    size = values.shape[0] // rows
    blocks = values.reshape(rows, size, cols, size) * pattern[:, None, :, None].astype(values.dtype)
    return blocks.reshape(rows * size, cols * size)


def add_blocks(matrix, stacked):
    size = stacked.shape[1]
    count = stacked.shape[0] // size
    eye_k = jnp.eye(count, dtype=jnp.float32)
    placed = stacked.reshape(count, size, size)[:, :, None, :] * eye_k[:, None, :, None]
    return matrix + placed.reshape(count * size, count * size)


def inner_rows(left, right):
    return lax.dot_general(
        left, right, (((0,), (0,)), ((), ())), preferred_element_type=jnp.float32
    )


def inner_exact(left, right):
    return lax.dot_general(
        left,
        right,
        (((0,), (0,)), ((), ())),
        precision=lax.Precision.HIGHEST,
        preferred_element_type=jnp.float32,
    )


def per_device(
    anc_inv,
    lower_one,
    pattern_one,
    pivot_one,
    lower_zero,
    pattern_zero,
    coupling_zero,
    pattern_couple,
    pivot_zero,
):
    upper = masked(lower_one, pattern_one)
    own_rows = anc_inv.shape[0]

    def fold_panel(total, piece):
        return total + jnp.dot(anc_inv, piece, preferred_element_type=jnp.float32)

    empty = jnp.zeros((own_rows, upper.shape[1]), jnp.float32)
    upper_sum = fold_panel(empty, lax.all_gather(upper, "row", axis=0, tiled=True))
    inv_cross = (-upper_sum).astype(jnp.bfloat16)
    pivot_part = inner_rows(upper, inv_cross)
    inv_pivot = add_blocks(-lax.psum(pivot_part, "row"), pivot_one)
    pivot_b = inv_pivot.astype(jnp.bfloat16)
    lower = masked(lower_zero, pattern_zero)
    coupling = masked(coupling_zero, pattern_couple)
    seeded = jnp.dot(inv_cross, coupling, preferred_element_type=jnp.float32)
    low_sum = fold_panel(seeded, lax.all_gather(lower, "row", axis=0, tiled=True))
    inv_low = (-low_sum).astype(jnp.bfloat16)
    coupling_part = inner_rows(inv_cross, lower)
    diag_part = inner_rows(lower, inv_low)
    coupling_wide = coupling.astype(jnp.float32)
    pivot_term = jnp.dot(pivot_b, coupling, preferred_element_type=jnp.float32)
    coupled = lax.psum(coupling_part, "row")
    inv_couple = -(coupled + pivot_term)
    diag_total = lax.psum(diag_part, "row")
    inv_diag = add_blocks(-(diag_total + inner_exact(coupling_wide, inv_couple)), pivot_zero)
    return (inv_cross, inv_pivot, inv_low, inv_couple, inv_diag)


def solution(mesh):
    placed = (
        P(("pole", "row"), None),
        P(("pole", "row"), None),
        P("row", None),
        P("pole", None),
        P(("pole", "row"), None),
        P("row", None),
        P("pole", None),
        P(),
        P("pole", None),
    )
    return jax.shard_map(
        per_device,
        mesh=mesh,
        in_specs=placed,
        out_specs=(
            P(("pole", "row"), None),
            P("pole", None),
            P(("pole", "row"), None),
            P("pole", None),
            P("pole", None),
        ),
        check_vma=False,
    )
```

profile of v0, /device:TPU:1, one launch (start us, length us, event | category | flops | bytes accessed | tf_op | source)
XLA Modules:
  0.0 240.7 jit_solution(9435690657850429769)
XLA Ops:
  7.2 0.0 copy-start
  7.2 0.0 all-gather.3.cloned.1.call-start
  7.2 0.7 convert_bitcast_fusion.1
  7.9 0.1 broadcast_bitcast_fusion
  8.0 1.6 broadcast_multiply_fusion.2
  9.6 0.0 all-gather.3.cloned.1.call-update
  9.7 0.0 all-gather.5.cloned.1.call-start
  9.7 0.7 convert_bitcast_fusion
  10.4 0.1 broadcast_bitcast_fusion.1
  10.4 1.6 broadcast_multiply_fusion.3
  12.0 0.0 copy-start.4
  12.0 0.0 all-gather.5.cloned.1.call-update
  12.0 0.0 all-reduce.3.cloned.1.call-start
  12.1 0.7 convert_element_type.58
  12.8 0.1 copy.17
  12.9 0.0 copy-start.2
  12.9 45.7 %all-gather.3.cloned.1.call-done = bf16[2048,768]{1,0:T(8,128)(2,1)} async-done(((bf16[128,768]{1,0:T(8,128)(2,1)}), bf16[2048,768]{1,0:T(8,128)(2,1)}) %all-gather.3.cloned.1.call-update) | async-done | bytes 3145744 | tf_op jit(solution)/shard_map/all_gather | solution.py:56
  58.6 0.0 copy-done
  58.6 2.9 %fusion.3 = bf16[768,128]{1,0:T(8,128)(2,1)S(1)} fusion(bf16[2048,768]{1,0:T(8,128)(2,1)} %all-gather.3.cloned.1.call-done, bf16[128,2048]{1,0:T(8,128)(2,1)S(1)} %copy-done), kind=kOutput, calls=%fused_computation.8 | convolution fusion | flops 402849792 | bytes 3866624 | tf_op jit(solution)/shard_map/dot_general | solution.py:53
  61.5 0.0 copy-done.4
  61.5 0.0 copy-start.5
  61.5 1.5 fusion.11
  63.0 0.3 mul.88
  63.3 0.0 copy-done.2
  63.3 0.3 fusion.9
  63.6 0.0 copy-done.5
  63.6 1.9 fusion.10
  65.5 36.0 %all-gather.5.cloned.1.call-done = bf16[2048,512]{1,0:T(8,128)(2,1)} async-done(((bf16[128,512]{1,0:T(8,128)(2,1)}), bf16[2048,512]{1,0:T(8,128)(2,1)}) %all-gather.5.cloned.1.call-update) | async-done | bytes 2097168 | tf_op jit(solution)/shard_map/all_gather | solution.py:64
  101.6 2.0 fusion.6
  103.6 0.0 copy-start.8
  103.6 1.3 fusion.12
  104.9 0.0 all-reduce.3.cloned.1.call-update
  105.0 0.0 copy-done.8
  105.0 1.2 broadcast_multiply_fusion.1
  106.2 2.9 %broadcast_multiply_fusion = f32[6,128,6,128]{3,2,1,0:T(8,128)} fusion(f32[6,6]{1,0:T(8,128)S(1)} %fusion.7, f32[6,128,128]{2,1,0:T(8,128)} %bitcast.52), kind=kLoop, calls=%fused_computation.2 | loop fusion | flops 589824 | bytes 2752656 | tf_op jit(solution)/shard_map/mul | solution.py:18
  109.1 0.8 copy.19
  109.9 116.1 %all-reduce.3.cloned.1.call-done = (f32[768,768]{1,0:T(8,128)}, f32[768,512]{1,0:T(8,128)}, f32[512,512]{1,0:T(8,128)}) async-done(((f32[768,768]{1,0:T(8,128)}, f32[768,512]{1,0:T(8,128)}, f32[512,512]{1,0:T(8,128)}), (f32[768,768]{1,0:T(8,128)}, f32[768,512]{1,0:T(8,128)}, f32[512,512]{1,0:T(8,128)})) %all-reduce.3.cloned.1.call-update) | async-done | bytes 4980752 | tf_op jit(solution)/shard_map/psum | solution.py:59
  226.0 0.0 copy-start.6
  226.0 3.5 %bitcast_add_fusion = f32[768,768]{1,0:T(8,128)S(1)} fusion(f32[96,8,6,128]{3,2,1,0:T(8,128)} %bitcast.49, f32[768,768]{1,0:T(8,128)} %get-tuple-element.15), kind=kLoop, calls=%fused_computation | loop fusion | flops 1179648 | bytes 7077888 | tf_op jit(solution)/shard_map/add | solution.py:19
  229.5 0.0 copy-start.1
  229.5 0.0 copy-done.6
  229.5 0.0 copy-start.7
  229.5 0.8 add_negate_fusion
  230.3 0.6 copy-done.1
  230.9 0.0 copy-start.3
  230.9 0.6 copy-done.7
  231.5 2.6 %fusion.1 = f32[512,512]{1,0:T(8,128)} fusion(f32[512,512]{1,0:T(8,128)S(1)} %copy-done.7, f32[768,512]{1,0:T(8,128)S(1)} %add_negate_fusion, f32[64,8,4,128]{3,2,1,0:T(4,128)S(1)} %bitcast.50, bf16[768,512]{1,0:T(8,128)(2,1)S(1)} %copy-done.2, bf16[96,8,4,128]{3,2,1,0:T(4,128)(2,1)S(1)} %bitcast.48), kind=kOutput, calls=%fused_computation.5 | convolution fusion | flops 2417098752 | bytes 6291456 | tf_op jit(solution)/shard_map/dot_general | solution.py:29
  234.2 0.0 copy-done.3
  (2 shorter events, 0.0 us)
Async XLA Ops:
  7.2 51.4 %copy-start = (bf16[128,2048]{1,0:T(8,128)(2,1)S(1)}, bf16[128,2048]{1,0:T(8,128)(2,1)}, u32[]{:S(2)}) copy-start(bf16[128,2048]{1,0:T(8,128)(2,1)} %param.9) | copy-start | bytes 1572868
  7.2 51.4 %all-gather.3.cloned.1.call-start = ((), (), s32[]{:S(2)}) async-start(), calls=%async_computation | async-start | bytes 3342336 | tf_op jit(solution)/shard_map/all_gather | solution.py:56
  9.7 91.9 %all-gather.5.cloned.1.call-start = ((), (), s32[]{:S(2)}) async-start(), calls=%async_computation.1 | async-start | bytes 2228224 | tf_op jit(solution)/shard_map/all_gather | solution.py:64
  12.0 49.5 %copy-start.4 = (bf16[128,512]{1,0:T(8,128)(2,1)S(1)}, bf16[128,512]{1,0:T(8,128)(2,1)}, u32[]{:S(2)}) copy-start(bf16[128,512]{1,0:T(8,128)(2,1)} %broadcast_multiply_fusion.3) | copy-start | bytes 393220
  12.0 214.0 %all-reduce.3.cloned.1.call-start = ((), (), s32[]{:S(2)}) async-start(), calls=%async_computation.2 | async-start | bytes 9961472 | tf_op jit(solution)/shard_map/psum | solution.py:59
  12.9 50.4 %copy-start.2 = (bf16[768,512]{1,0:T(8,128)(2,1)S(1)}, bf16[768,512]{1,0:T(8,128)(2,1)}, u32[]{:S(2)}) copy-start(bf16[768,512]{1,0:T(8,128)(2,1)} %param.15) | copy-start | bytes 2359300
  61.5 2.1 copy-start.5
  103.6 1.3 copy-start.8
  226.0 3.5 %copy-start.6 = (f32[768,512]{1,0:T(8,128)S(1)}, f32[768,512]{1,0:T(8,128)}, u32[]{:S(2)}) copy-start(f32[768,512]{1,0:T(8,128)} %get-tuple-element.16) | copy-start | bytes 4718596
  229.5 1.4 copy-start.1
  229.5 2.0 copy-start.7
  230.9 3.3 %copy-start.3 = (f32[768,512]{1,0:T(8,128)}, f32[768,512]{1,0:T(8,128)S(1)}, u32[]{:S(2)}) copy-start(f32[768,512]{1,0:T(8,128)S(1)} %add_negate_fusion) | copy-start | bytes 4718596
Sparse Core Ops, SparseCore 0:
  10.9 47.6 all-gather.2
  61.3 40.2 all-gather.4
  106.1 119.8 all-reduce.2
where the time goes:
time: 242 us; the launch traced here: 241 us
  waiting for transfers between devices  198 us (82%)
  between operations  13.9 us (6%)
  matrix products  13.4 us (6%)
  other arithmetic  12.8 us (5%)
  local copies, waits for them, and re-layouts  2.6 us (1%)
    psum x1, waiting for transfers between devices, per_device(): inv_pivot = add_blocks(-lax.psum(pivot_part, 'row'), pivot_one)  116 us
    all_gather x1, waiting for transfers between devices, per_device(): lax.all_gather(upper, 'row', axis=0, tiled=True)  45.7 us
    all_gather x1, waiting for transfers between devices, per_device(): lax.all_gather(lower, 'row', axis=0, tiled=True)  36 us
    dot_general x2, matrix products, fold_panel(): return total + jnp.dot(anc_inv, piece, preferred_element_type=jnp.float32)  4.95 us
  transfers between devices with their start and end apart: 3, of which 3 were waited for; matrix products, arithmetic and copies ran while one was open for 6% of the time, Pallas kernels for 0%

commit v1 on v0

v1 whole, which is shorter than its diff:
```python
import functools

import jax
import jax.numpy as jnp
from jax import lax
from jax.experimental import pallas as pl
from jax.experimental.pallas import tpu as pltpu
from jax.sharding import PartitionSpec as P

F32 = jnp.float32
BF16 = jnp.bfloat16
MESH = pl.DeviceIdType.MESH


def mul(a, b):
    return jnp.dot(a, b, preferred_element_type=F32)


def mul_t(a, b):
    return lax.dot_general(a, b, (((0,), (0,)), ((), ())), preferred_element_type=F32)


def kernel(
    n, snake, k1, k0, size,
    anc, l_one, pat_one, piv_one, l_zero, pat_zero, couple, pat_couple, piv_zero,
    o_cross, o_pivot, o_low, o_couple, o_diag,
    up, lo, x_up, x_lo, part, sib_part, half, from_left, from_right, out_left, out_right, total,
    ag_send, ag_recv, sib_send, sib_recv, pair_send, pair_recv,
    rs_send, rs_recv, fin_send, fin_recv, fs_send, fs_recv,
):
    chips = n // 2
    far = chips // 2
    blocks = k1 + k0
    rows = size
    me = lax.axis_index("row")
    core = me % 2
    chip = me // 2

    def chip_at(q):
        q = (q + chips) % chips
        if not snake:
            return q
        h = q // far
        return (1 - h) * 2 * q + h * (2 * (chips - 1 - q) + 1)

    if snake:
        y = chip % 2
        z = chip // 2
        pos = z * (1 - y) + (chips - 1 - z) * y
    else:
        pos = chip
    right = chip_at(pos + 1) * 2 + core
    left = chip_at(pos - 1) * 2 + core
    sib = chip * 2 + (1 - core)

    barrier = pltpu.get_barrier_semaphore()
    for other in (left, right, sib):
        pl.semaphore_signal(barrier, inc=1, device_id={"row": other}, device_id_type=MESH)

    own = pl.ds(pl.multiple_of(me * rows, rows), rows)
    for j in range(k1):
        cols = slice(j * size, (j + 1) * size)
        up[own, cols] = (l_one[:, cols].astype(F32) * pat_one[0, j].astype(F32)).astype(BF16)
    for j in range(k0):
        cols = slice(j * size, (j + 1) * size)
        lo[own, cols] = (l_zero[:, cols].astype(F32) * pat_zero[0, j].astype(F32)).astype(BF16)
    pl.semaphore_wait(barrier, 3)

    bufs = (up, lo)

    def copy(src, dst, ss, rs, target):
        return pltpu.make_async_remote_copy(
            src_ref=src, dst_ref=dst, send_sem=ss, recv_sem=rs,
            device_id={"row": target}, device_id_type=MESH)

    pending = []

    def block(ch, q, kk):
        r = chip_at(q) * 2 + kk
        return bufs[ch].at[pl.ds(pl.multiple_of(r * rows, rows), rows), :]

    def origin(d, s):
        return pos - s if d == 0 else pos + s

    def ring(d, s, ch, q):
        ref = block(ch, q, core)
        return copy(ref, ref, ag_send.at[d, s, ch], ag_recv.at[d, s, ch], right if d == 0 else left)

    def pair(d, s, ch, kk):
        ref = block(ch, origin(d, s), kk)
        return copy(ref, ref, sib_send.at[d, s, ch], sib_recv.at[d, s, ch], sib)

    def active(d, s, ch):
        return s < far or (s == far and ch == d)

    def start(c):
        c.start()
        pending.append(c)

    for ch in range(2):
        for d in range(2):
            if active(d, 1, ch):
                start(ring(d, 1, ch, pos))
    for ch in range(2):
        start(pair(0, 0, ch, core))

    def add(ch, q, first=False):
        c = chip_at(q)
        cols = pl.ds(pl.multiple_of(c * 2 * rows, 2 * rows), 2 * rows)
        acc = (x_up, x_lo)[ch]
        term = mul(anc[:, cols], bufs[ch][cols, :])
        if first:
            acc[...] = term
        else:
            acc[...] += term

    def settle(s):
        for ch in range(2):
            for d in range(2):
                if (s == 0 and d == 0) or (s > 0 and active(d, s, ch)):
                    pair(d, s, ch, 1 - core).wait_recv()
                    add(ch, origin(d, s), s == 0)

    for s in range(1, far + 1):
        for ch in range(2):
            for d in range(2):
                if active(d, s, ch):
                    ring(d, s, ch, origin(d, s)).wait_recv()
                    if active(d, s + 1, ch):
                        start(ring(d, s + 1, ch, origin(d, s)))
                    start(pair(d, s, ch, core))
        settle(s - 1)
    settle(far)

    xb_up = x_up[...].astype(BF16)
    xb_lo = x_lo[...].astype(BF16)
    o_cross[...] = -xb_up
    own_l = jnp.concatenate([up[own, :], lo[own, :]], axis=1)
    xb = jnp.concatenate([xb_up, xb_lo], axis=1)

    where = {}
    at = 0
    for i in range(blocks):
        g = mul_t(xb[:, i * size:(i + 1) * size], own_l[:, i * size:])
        for j in range(i, blocks):
            where[i, j] = at
            part[at * size:(at + 1) * size, :] = g[:, (j - i) * size:(j - i + 1) * size].astype(BF16)
            at += 1
    packed = part.shape[0]
    if at * size < packed:
        part[at * size:, :] = jnp.zeros((packed - at * size, size), BF16)
    hrows = packed // 2
    piece = hrows // chips

    def half_at(kk):
        return pl.ds(pl.multiple_of(kk * hrows, hrows), hrows)

    swap = copy(part.at[half_at(1 - core), :], sib_part, pair_send, pair_recv, sib)
    start(swap)

    lk = [[None] * k0 for _ in range(k1)]
    for i in range(k1):
        for j in range(k0):
            lk[i][j] = (couple[i * size:(i + 1) * size, j * size:(j + 1) * size].astype(F32)
                        * pat_couple[i, j].astype(F32)).astype(BF16)
    lkm = jnp.concatenate([jnp.concatenate(r, axis=1) for r in lk], axis=0)
    o_low[...] = (-(x_lo[...] - mul(xb_up, lkm))).astype(BF16)

    swap.wait_recv()
    half[...] = part[half_at(core), :].astype(F32) + sib_part[...].astype(F32)

    def of_piece(q):
        q = (q + chips) % chips
        return pl.ds(pl.multiple_of(q * piece, piece), piece)

    outs = (out_right, out_left)
    ins = (from_left, from_right)
    reach = (far, chips - 1 - far)

    def rs(d, s):
        return copy(outs[d].at[s - 1], ins[d].at[s - 1], rs_send.at[d, s], rs_recv.at[d, s],
                    right if d == 0 else left)

    for s in range(1, far + 1):
        for d in range(2):
            if s > reach[d]:
                continue
            q = pos + (reach[d] - s + 1) * (1 if d == 0 else -1)
            value = half[of_piece(q), :]
            if s > 1:
                rs(d, s - 1).wait_recv()
                value = value + ins[d][s - 2].astype(F32)
            outs[d][s - 1] = value.astype(BF16)
            start(rs(d, s))
    value = half[of_piece(pos), :]
    for d in range(2):
        rs(d, reach[d]).wait_recv()
        value = value + ins[d][reach[d] - 1].astype(F32)
    cut = (piece // 32) * 16
    spans = ((0, cut), (cut, piece - cut))
    total[pl.ds(pl.multiple_of(core * hrows + pos * piece, 16), piece), :] = value.astype(BF16)

    def fin_block(ch, q, kk):
        q = (q + chips) % chips
        off, count = spans[ch]
        return total.at[pl.ds(pl.multiple_of(kk * hrows + q * piece + off, 16), count), :]

    def fin(d, s, ch, q):
        ref = fin_block(ch, q, core)
        return copy(ref, ref, fin_send.at[d, s, ch], fin_recv.at[d, s, ch], right if d == 0 else left)

    def fin_pair(d, s, ch, kk):
        ref = fin_block(ch, origin(d, s), kk)
        return copy(ref, ref, fs_send.at[d, s, ch], fs_recv.at[d, s, ch], sib)

    for ch in range(2):
        for d in range(2):
            if active(d, 1, ch):
                start(fin(d, 1, ch, pos))
    for ch in range(2):
        start(fin_pair(0, 0, ch, core))
    for s in range(1, far + 1):
        for ch in range(2):
            for d in range(2):
                if active(d, s, ch):
                    fin(d, s, ch, origin(d, s)).wait_recv()
                    if active(d, s + 1, ch):
                        start(fin(d, s + 1, ch, origin(d, s)))
                    start(fin_pair(d, s, ch, core))
    for s in range(far + 1):
        for ch in range(2):
            for d in range(2):
                if (s == 0 and d == 0) or (s > 0 and active(d, s, ch)):
                    fin_pair(d, s, ch, 1 - core).wait_recv()

    def tri(i, j):
        b = where[i, j]
        return total[b * size:(b + 1) * size, :].astype(F32)

    for i in range(k1):
        for j in range(i, k1):
            g = tri(i, j)
            ri, rj = slice(i * size, (i + 1) * size), slice(j * size, (j + 1) * size)
            if i == j:
                o_pivot[ri, rj] = g + piv_one[ri, :]
            else:
                o_pivot[ri, rj] = g
                o_pivot[rj, ri] = g.T
    pivot_b = o_pivot[...].astype(BF16)
    cross = jnp.concatenate(
        [jnp.concatenate([total[where[i, k1 + j] * size:(where[i, k1 + j] + 1) * size, :] for j in range(k0)], axis=1)
         for i in range(k1)], axis=0)
    coupled = cross.astype(F32) - mul(pivot_b, lkm)
    o_couple[...] = coupled
    high = coupled.astype(BF16)
    low = (coupled - high.astype(F32)).astype(BF16)
    update = mul_t(cross, lkm) + mul_t(lkm, high) + mul_t(lkm, low)
    for i in range(k0):
        for j in range(i, k0):
            g = tri(k1 + i, k1 + j)
            ri, rj = slice(i * size, (i + 1) * size), slice(j * size, (j + 1) * size)
            if i == j:
                o_diag[ri, rj] = g + piv_zero[ri, :] - update[ri, rj]
            else:
                o_diag[ri, rj] = g - update[ri, rj]
                o_diag[rj, ri] = g.T - update[rj, ri]

    for c in pending:
        c.wait_send()


def per_device(n, snake, *args):
    anc, l_one, pat_one, piv_one, l_zero, pat_zero, couple, pat_couple, piv_zero = args
    rows, order = anc.shape
    size = piv_one.shape[1]
    w1, w0 = l_one.shape[1], l_zero.shape[1]
    k1, k0 = w1 // size, w0 // size
    blocks = k1 + k0
    tri = blocks * (blocks + 1) // 2 * size
    unit = 16 * n
    packed = -(-tri // unit) * unit
    chips = n // 2
    far = chips // 2
    piece = packed // n
    vmem = pl.BlockSpec(memory_space=pltpu.VMEM)
    smem = pl.BlockSpec(memory_space=pltpu.SMEM)
    dma = pltpu.SemaphoreType.DMA
    return pl.pallas_call(
        functools.partial(kernel, n, snake, k1, k0, size),
        out_shape=(
            jax.ShapeDtypeStruct((rows, w1), BF16),
            jax.ShapeDtypeStruct((w1, w1), F32),
            jax.ShapeDtypeStruct((rows, w0), BF16),
            jax.ShapeDtypeStruct((w1, w0), F32),
            jax.ShapeDtypeStruct((w0, w0), F32),
        ),
        in_specs=[vmem, vmem, smem, vmem, vmem, smem, vmem, smem, vmem],
        out_specs=(vmem,) * 5,
        scratch_shapes=[
            pltpu.VMEM((order, w1), BF16),
            pltpu.VMEM((order, w0), BF16),
            pltpu.VMEM((rows, w1), F32),
            pltpu.VMEM((rows, w0), F32),
            pltpu.VMEM((packed, size), BF16),
            pltpu.VMEM((packed // 2, size), BF16),
            pltpu.VMEM((packed // 2, size), F32),
            pltpu.VMEM((far, piece, size), BF16),
            pltpu.VMEM((far, piece, size), BF16),
            pltpu.VMEM((far, piece, size), BF16),
            pltpu.VMEM((far, piece, size), BF16),
            pltpu.VMEM((packed, size), BF16),
            dma((2, far + 1, 2)), dma((2, far + 1, 2)),
            dma((2, far + 1, 2)), dma((2, far + 1, 2)),
            dma, dma,
            dma((2, far + 1)), dma((2, far + 1)),
            dma((2, far + 1, 2)), dma((2, far + 1, 2)),
            dma((2, far + 1, 2)), dma((2, far + 1, 2)),
        ],
        compiler_params=pltpu.CompilerParams(
            collective_id=0, has_side_effects=True, vmem_limit_bytes=56 * 1024 * 1024),
    )(*args)


def solution(mesh):
    n = mesh.shape["row"]
    placed = (
        P(("pole", "row"), None),
        P(("pole", "row"), None),
        P("row", None),
        P("pole", None),
        P(("pole", "row"), None),
        P("row", None),
        P("pole", None),
        P(),
        P("pole", None),
    )
    return jax.shard_map(
        functools.partial(per_device, n, n == 16),
        mesh=mesh,
        in_specs=placed,
        out_specs=(
            P(("pole", "row"), None),
            P("pole", None),
            P(("pole", "row"), None),
            P("pole", None),
            P("pole", None),
        ),
        check_vma=False,
    )
```

time: 242 us -> 86.7 us (0.36)
  waiting for transfers between devices: 198 us -> 0 us
  Pallas kernels: 0 us -> 76.8 us
  matrix products: 13.4 us -> 0 us
  between operations: 13.9 us -> 0.64 us
  other arithmetic: 12.8 us -> 0 us
  local copies, waits for them, and re-layouts: 2.6 us -> 9.1 us
    psum x1 -> x0, waiting for transfers between devices: 116 us -> none  [per_device(): inv_pivot = add_blocks(-lax.psum(pivot_part, 'row'), pivot_one)]
    all_gather x2 -> x0, waiting for transfers between devices: 81.7 us -> none  [the longest x1 45.7 us: per_device(): lax.all_gather(upper, 'row', axis=0, tiled=True)]
    pallas_call x0 -> x1, Pallas kernels: none -> 76.8 us  [per_device(): pl.pallas_call(functools.partial(kernel, n, snake, k1, k0, size), out_sha...]
    dot_general x8 -> x0, matrix products: 13.4 us -> none  [the longest x2 4.95 us: fold_panel(): return total + jnp.dot(anc_inv, piece, preferred_element_type=jnp.float32)]
    mul x4 -> x0, other arithmetic: 7.32 us -> none  [the longest x2 4.13 us: add_blocks(): stacked.reshape(count, size, size)[:, :, None, :] * eye_k[:, None, :, None]]
    unnamed x19 -> x12, local copies, waits for them, and re-layouts: 2.07 us -> 9.1 us
    add x1 -> x0, other arithmetic: 3.46 us -> none  [add_blocks(): return matrix + placed.reshape(count * size, count * size)]
  transfers between devices with their start and end apart: 3 -> 0, of which waited for: 3 -> 0; matrix products, arithmetic and copies ran while one was open for 6% -> 0% of each run, Pallas kernels for 0% -> 0%
where the time goes in v1:
time: 86.7 us; the launch traced here: 86.5 us
  Pallas kernels  76.8 us (89%)
  local copies, waits for them, and re-layouts  9.1 us (10%)
    pallas_call x1, Pallas kernels, per_device(): pl.pallas_call(functools.partial(kernel, n, snake, k1, k0, size), out_sha...  76.8 us
    unnamed x12, local copies, waits for them, and re-layouts  9.1 us

profile of v1, /device:TPU:1, one launch (start us, length us, event | category | flops | bytes accessed | tf_op | source)
XLA Modules:
  0.0 86.5 jit_solution(13839284037071040120)
XLA Ops:
  0.6 1.4 %copy.14.pat_couple = s32[6,4]{1,0:T(8,128)} copy(s32[6,4]{0,1:T(4,128)} %param.16) | data formatting | bytes 192 | tf_op args[7]
  2.0 76.8 %shard_map.128 = (bf16[128,768]{1,0:T(8,128)(2,1)}, f32[768,768]{1,0:T(8,128)}, bf16[128,512]{1,0:T(8,128)(2,1)}, f32[768,512]{1,0:T(8,128)}, f32[512,512]{1,0:T(8,128)}) custom-call(bf16[128,2048]{1,0:T(8,128)(2,1)} %anc.1, bf16[128,768]{1,0:T(8,128)(2,1)} %l_one.1, s32[1,6]{1,0:T(1,128)} %pat_one.1, f32[768,128]{1,0:T(8,128)} %piv_one.1, ...), custom_call_target="tpu_custom_call" | custom-call | tf_op jit(solution)/shard_map/pallas_call | solution.py:288
  78.7 1.6 %copy.20 = bf16[128,768]{1,0:T(8,128)(2,1)} copy(bf16[128,768]{1,0:T(8,128)(2,1)} %get-tuple-element.10) | data formatting | bytes 393216
  80.4 0.0 copy-start.2
  80.4 0.0 copy-start
  80.4 3.3 %copy.21 = f32[768,768]{1,0:T(8,128)} copy(f32[768,768]{1,0:T(8,128)} %get-tuple-element.11) | data formatting | bytes 4718592
  83.7 0.0 copy-done.2
  83.7 0.0 copy-start.1
  83.7 0.7 copy.22
  84.4 0.0 copy-done
  84.4 1.1 %copy.23 = f32[768,512]{1,0:T(8,128)} copy(f32[768,512]{1,0:T(8,128)S(1)} %copy-done) | data formatting | bytes 3145728
  85.5 0.0 copy-done.1
  85.5 1.0 %copy.24 = f32[512,512]{1,0:T(8,128)} copy(f32[512,512]{1,0:T(8,128)S(1)} %copy-done.1) | data formatting | bytes 2097152
Async XLA Ops:
  80.4 3.4 %copy-start.2 = (bf16[128,512]{1,0:T(8,128)(2,1)S(1)}, bf16[128,512]{1,0:T(8,128)(2,1)}, u32[]{:S(2)}) copy-start(bf16[128,512]{1,0:T(8,128)(2,1)} %get-tuple-element.12) | copy-start | bytes 393220
  80.4 4.0 %copy-start = (f32[768,512]{1,0:T(8,128)S(1)}, f32[768,512]{1,0:T(8,128)}, u32[]{:S(2)}) copy-start(f32[768,512]{1,0:T(8,128)} %get-tuple-element.13) | copy-start | bytes 4718596
  83.7 1.8 %copy-start.1 = (f32[512,512]{1,0:T(8,128)S(1)}, f32[512,512]{1,0:T(8,128)}, u32[]{:S(2)}) copy-start(f32[512,512]{1,0:T(8,128)} %get-tuple-element.14) | copy-start | bytes 3145732

commit v2 on v0

v2 whole, which is shorter than its diff:
```python
import functools

import jax
import jax.numpy as jnp
from jax import lax
from jax.experimental import pallas as pl
from jax.experimental.pallas import tpu as pltpu
from jax.sharding import PartitionSpec as P

F32 = jnp.float32
BF16 = jnp.bfloat16
MESH = pl.DeviceIdType.MESH


def mul(a, b):
    return jnp.dot(a, b, preferred_element_type=F32)


def mul_t(a, b):
    return lax.dot_general(a, b, (((0,), (0,)), ((), ())), preferred_element_type=F32)


def kernel(
    n, snake, k1, k0, size, lags,
    anc, l_one, pat_one, l_zero, pat_zero,
    o_x0, o_x1, o_x2, tot0, tot1, tot2,
    l0_ref, l1_ref, l2_ref, acc0, acc1, acc2,
    part0, part1, part2, sib0, sib1, sib2, half0, half1, half2,
    in0, in1, in2, out0, out1, out2,
    ag_send, ag_recv, sib_send, sib_recv, pair_send, pair_recv,
    rs_send, rs_recv, fin_send, fin_recv, fs_send, fs_recv,
):
    chips = n // 2
    far = chips // 2
    rows = size
    me = lax.axis_index("row")
    core = me % 2
    chip = me // 2

    def chip_at(q):
        q = (q + chips) % chips
        if not snake:
            return q
        h = q // far
        return (1 - h) * 2 * q + h * (2 * (chips - 1 - q) + 1)

    if snake:
        y = chip % 2
        z = chip // 2
        pos = z * (1 - y) + (chips - 1 - z) * y
    else:
        pos = chip
    right = chip_at(pos + 1) * 2 + core
    left = chip_at(pos - 1) * 2 + core
    sib = chip * 2 + (1 - core)

    barrier = pltpu.get_barrier_semaphore()
    for other in (left, right, sib):
        pl.semaphore_signal(barrier, inc=1, device_id={"row": other}, device_id_type=MESH)

    groups = column_groups(k1, k0)
    bufs = (l0_ref, l1_ref, l2_ref)
    accs = (acc0, acc1, acc2)
    xouts = (o_x0, o_x1, o_x2)
    parts, sibs, halves = (part0, part1, part2), (sib0, sib1, sib2), (half0, half1, half2)
    ins, outs, tots = (in0, in1, in2), (out0, out1, out2), (tot0, tot1, tot2)

    own = pl.ds(pl.multiple_of(me * rows, rows), rows)
    for g, cols in enumerate(groups):
        for at, j in enumerate(cols):
            if j < k1:
                value = l_one[:, j * size:(j + 1) * size].astype(F32) * pat_one[0, j].astype(F32)
            else:
                j -= k1
                value = l_zero[:, j * size:(j + 1) * size].astype(F32) * pat_zero[0, j].astype(F32)
            bufs[g][own, at * size:(at + 1) * size] = value.astype(BF16)
    pl.semaphore_wait(barrier, 3)

    pending = []

    def copy(src, dst, ss, rs, target):
        return pltpu.make_async_remote_copy(
            src_ref=src, dst_ref=dst, send_sem=ss, recv_sem=rs,
            device_id={"row": target}, device_id_type=MESH)

    def start(c):
        c.start()
        pending.append(c)

    def towards(d):
        return right if d == 0 else left

    def origin(d, s):
        return pos - s if d == 0 else pos + s

    def span(d, s, count):
        cut = count // 32 * 16
        if s < far:
            return 0, count
        return (0, cut) if d == 0 else (cut, count - cut)

    def task(g):
        buf, acc, part, half, tot = bufs[g], accs[g], parts[g], halves[g], tots[g]
        hrows = part.shape[0] // 2
        piece = hrows // chips

        def gathered(view, count, send, recv, fsend, frecv):
            def ring(d, s, q):
                ref = view(q, core, *span(d, s, count))
                return copy(ref, ref, send.at[g, d, s], recv.at[g, d, s], towards(d))

            def pair(d, s, kk):
                ref = view(origin(d, s), kk, *span(d, s, count))
                return copy(ref, ref, fsend.at[g, d, s], frecv.at[g, d, s], sib)

            return ring, pair

        def block(q, kk, off, count):
            r = chip_at(q) * 2 + kk
            return buf.at[pl.ds(pl.multiple_of(r * rows + off, 16), count), :]

        def add(q, first=False):
            c = chip_at(q)
            cols = pl.ds(pl.multiple_of(c * 2 * rows, 2 * rows), 2 * rows)
            term = mul(anc[:, cols], buf[cols, :])
            if first:
                acc[...] = term
            else:
                acc[...] += term

        ring, pair = gathered(block, rows, ag_send, ag_recv, sib_send, sib_recv)
        for d in range(2):
            start(ring(d, 1, pos))
        start(pair(0, 0, core))
        yield
        for s in range(1, far + 1):
            for d in range(2):
                ring(d, s, origin(d, s)).wait_recv()
                if s < far:
                    start(ring(d, s + 1, origin(d, s)))
                start(pair(d, s, core))
            if s == 1:
                pair(0, 0, 1 - core).wait_recv()
                add(pos, True)
            else:
                for d in range(2):
                    pair(d, s - 1, 1 - core).wait_recv()
                    add(origin(d, s - 1))
            if s < far:
                yield
        for d in range(2):
            pair(d, far, 1 - core).wait_recv()
        add(pos + far)

        x = acc[...]
        xb = x.astype(BF16)
        xouts[g][...] = x.astype(xouts[g].dtype)
        own_l = jnp.concatenate([b[own, :] for b in bufs[g:]], axis=1)
        at = 0
        for i in range(len(groups[g])):
            prod = mul_t(xb[:, i * size:(i + 1) * size], own_l[:, i * size:]).astype(BF16)
            for j in range(prod.shape[1] // size):
                part[at * size:(at + 1) * size, :] = prod[:, j * size:(j + 1) * size]
                at += 1
        if at * size < part.shape[0]:
            part[at * size:, :] = jnp.zeros((part.shape[0] - at * size, size), BF16)

        def half_at(kk):
            return pl.ds(pl.multiple_of(kk * hrows, 16), hrows)

        swap = copy(part.at[half_at(1 - core), :], sibs[g], pair_send.at[g], pair_recv.at[g], sib)
        start(swap)
        yield

        swap.wait_recv()
        half[...] = part[half_at(core), :].astype(F32) + sibs[g][...].astype(F32)

        def of_piece(q):
            q = (q + chips) % chips
            return pl.ds(pl.multiple_of(q * piece, 16), piece)

        reach = (far, chips - 1 - far) if g == 0 else (chips - 1 - far, far)

        def rs(d, s):
            return copy(outs[g].at[d, s - 1], ins[g].at[d, s - 1], rs_send.at[g, d, s], rs_recv.at[g, d, s],
                        towards(d))

        for s in range(1, far + 1):
            for d in range(2):
                if s > reach[d]:
                    continue
                q = pos + (reach[d] - s + 1) * (1 if d == 0 else -1)
                value = half[of_piece(q), :]
                if s > 1:
                    rs(d, s - 1).wait_recv()
                    value = value + ins[g][d, s - 2].astype(F32)
                outs[g][d, s - 1] = value.astype(BF16)
                start(rs(d, s))
            yield
        value = half[of_piece(pos), :]
        for d in range(2):
            rs(d, reach[d]).wait_recv()
            value = value + ins[g][d, reach[d] - 1].astype(F32)
        tot[pl.ds(pl.multiple_of(core * hrows + pos * piece, 16), piece), :] = value.astype(BF16)

        def done(q, kk, off, count):
            q = (q + chips) % chips
            return tot.at[pl.ds(pl.multiple_of(kk * hrows + q * piece + off, 16), count), :]

        ring, pair = gathered(done, piece, fin_send, fin_recv, fs_send, fs_recv)
        for d in range(2):
            start(ring(d, 1, pos))
        start(pair(0, 0, core))
        yield
        for s in range(1, far + 1):
            for d in range(2):
                ring(d, s, origin(d, s)).wait_recv()
                if s < far:
                    start(ring(d, s + 1, origin(d, s)))
                start(pair(d, s, core))
            yield
        pair(0, 0, 1 - core).wait_recv()
        for s in range(1, far + 1):
            for d in range(2):
                pair(d, s, 1 - core).wait_recv()

    running = {g: task(g) for g in range(3)}
    tick = 0
    while running:
        for g in list(running):
            if tick >= lags[g] and next(running[g], "end") == "end":
                del running[g]
        tick += 1

    for c in pending:
        c.wait_send()


def column_groups(k1, k0):
    return (tuple(range(k1 // 2)), tuple(range(k1 // 2, k1)), tuple(range(k1, k1 + k0)))


def finish(
    k1, k0, size,
    x0, x1, x2, tot0, tot1, tot2, piv_one, couple, pat_couple, piv_zero,
    o_cross, o_pivot, o_low, o_couple, o_diag,
):
    where = {}
    for g, cols in enumerate(column_groups(k1, k0)):
        at = 0
        for i in cols:
            for j in range(i, k1 + k0):
                where[i, j] = (tot0, tot1, tot2)[g], at
                at += 1

    def tri(i, j):
        ref, b = where[i, j]
        return ref[b * size:(b + 1) * size, :]

    lkm = jnp.concatenate([
        jnp.concatenate([
            (couple[i * size:(i + 1) * size, j * size:(j + 1) * size].astype(F32)
             * jnp.broadcast_to(pat_couple[i:i + 1, j:j + 1].astype(F32), (size, size))).astype(BF16)
            for j in range(k0)], axis=1) for i in range(k1)], axis=0)

    for i in range(k1):
        for j in range(i, k1):
            g = tri(i, j).astype(F32)
            ri, rj = slice(i * size, (i + 1) * size), slice(j * size, (j + 1) * size)
            if i == j:
                o_pivot[ri, rj] = g + piv_one[ri, :]
            else:
                o_pivot[ri, rj] = g
                o_pivot[rj, ri] = g.T
    xb = jnp.concatenate([x0[...], x1[...]], axis=1)
    o_cross[...] = -xb
    o_low[...] = (mul(xb, lkm) - x2[...]).astype(BF16)
    pivot_b = o_pivot[...].astype(BF16)
    cross = jnp.concatenate(
        [jnp.concatenate([tri(i, k1 + j) for j in range(k0)], axis=1) for i in range(k1)], axis=0)
    coupled = cross.astype(F32) - mul(pivot_b, lkm)
    o_couple[...] = coupled
    high = coupled.astype(BF16)
    low = (coupled - high.astype(F32)).astype(BF16)
    update = mul_t(cross, lkm) + mul_t(lkm, high) + mul_t(lkm, low)
    for i in range(k0):
        for j in range(i, k0):
            g = tri(k1 + i, k1 + j).astype(F32)
            ri, rj = slice(i * size, (i + 1) * size), slice(j * size, (j + 1) * size)
            if i == j:
                o_diag[ri, rj] = g + piv_zero[ri, :] - update[ri, rj]
            else:
                o_diag[ri, rj] = g - update[ri, rj]
                o_diag[rj, ri] = g.T - update[rj, ri]


LAGS = (0, 1, 2)


def per_device(n, snake, *args):
    anc, l_one, pat_one, piv_one, l_zero, pat_zero, couple, pat_couple, piv_zero = args
    rows, order = anc.shape
    size = piv_one.shape[1]
    w1, w0 = l_one.shape[1], l_zero.shape[1]
    k1, k0 = w1 // size, w0 // size
    far = n // 4
    groups = column_groups(k1, k0)
    widths = [len(g) * size for g in groups]
    unit = 16 * n
    packed = [-(-sum(k1 + k0 - i for i in g) * size // unit) * unit for g in groups]
    vmem = pl.BlockSpec(memory_space=pltpu.VMEM)
    smem = pl.BlockSpec(memory_space=pltpu.SMEM)
    dma = pltpu.SemaphoreType.DMA
    steps = dma((3, 2, far + 1))
    limit = 56 * 1024 * 1024
    sums = pl.pallas_call(
        functools.partial(kernel, n, snake, k1, k0, size, LAGS),
        out_shape=(
            jax.ShapeDtypeStruct((rows, widths[0]), BF16),
            jax.ShapeDtypeStruct((rows, widths[1]), BF16),
            jax.ShapeDtypeStruct((rows, widths[2]), F32),
            *(jax.ShapeDtypeStruct((p, size), BF16) for p in packed),
        ),
        in_specs=[vmem, vmem, smem, vmem, smem],
        out_specs=(vmem,) * 6,
        scratch_shapes=[
            *(pltpu.VMEM((order, w), BF16) for w in widths),
            *(pltpu.VMEM((rows, w), F32) for w in widths),
            *(pltpu.VMEM((p, size), BF16) for p in packed),
            *(pltpu.VMEM((p // 2, size), BF16) for p in packed),
            *(pltpu.VMEM((p // 2, size), F32) for p in packed),
            *(pltpu.VMEM((2, far, p // n, size), BF16) for p in packed),
            *(pltpu.VMEM((2, far, p // n, size), BF16) for p in packed),
            steps, steps, steps, steps,
            dma((3,)), dma((3,)),
            steps, steps, steps, steps, steps, steps,
        ],
        compiler_params=pltpu.CompilerParams(
            collective_id=0, has_side_effects=True, vmem_limit_bytes=limit),
    )(anc, l_one, pat_one, l_zero, pat_zero)
    return pl.pallas_call(
        functools.partial(finish, k1, k0, size),
        out_shape=(
            jax.ShapeDtypeStruct((rows, w1), BF16),
            jax.ShapeDtypeStruct((w1, w1), F32),
            jax.ShapeDtypeStruct((rows, w0), BF16),
            jax.ShapeDtypeStruct((w1, w0), F32),
            jax.ShapeDtypeStruct((w0, w0), F32),
        ),
        in_specs=[vmem] * 10,
        out_specs=(vmem,) * 5,
        compiler_params=pltpu.CompilerParams(vmem_limit_bytes=limit),
    )(*sums, piv_one, couple, pat_couple, piv_zero)


def solution(mesh):
    n = mesh.shape["row"]
    placed = (
        P(("pole", "row"), None),
        P(("pole", "row"), None),
        P("row", None),
        P("pole", None),
        P(("pole", "row"), None),
        P("row", None),
        P("pole", None),
        P(),
        P("pole", None),
    )
    return jax.shard_map(
        functools.partial(per_device, n, n == 16),
        mesh=mesh,
        in_specs=placed,
        out_specs=(
            P(("pole", "row"), None),
            P("pole", None),
            P(("pole", "row"), None),
            P("pole", None),
            P("pole", None),
        ),
        check_vma=False,
    )
```

time: 242 us -> 77.3 us (0.32)
  waiting for transfers between devices: 198 us -> 0 us
  Pallas kernels: 0 us -> 75.1 us
  matrix products: 13.4 us -> 0 us
  between operations: 13.9 us -> 0.64 us
  other arithmetic: 12.8 us -> 0 us
    psum x1 -> x0, waiting for transfers between devices: 116 us -> none  [per_device(): inv_pivot = add_blocks(-lax.psum(pivot_part, 'row'), pivot_one)]
    all_gather x2 -> x0, waiting for transfers between devices: 81.7 us -> none  [the longest x1 45.7 us: per_device(): lax.all_gather(upper, 'row', axis=0, tiled=True)]
    pallas_call x0 -> x2, Pallas kernels: none -> 75.1 us  [the longest x1 69.8 us: per_device(): pl.pallas_call(functools.partial(kernel, n, snake, k1, k0, size, LAGS), o...]
    dot_general x8 -> x0, matrix products: 13.4 us -> none  [the longest x2 4.95 us: fold_panel(): return total + jnp.dot(anc_inv, piece, preferred_element_type=jnp.float32)]
    mul x4 -> x0, other arithmetic: 7.32 us -> none  [the longest x2 4.13 us: add_blocks(): stacked.reshape(count, size, size)[:, :, None, :] * eye_k[:, None, :, None]]
    add x1 -> x0, other arithmetic: 3.46 us -> none  [add_blocks(): return matrix + placed.reshape(count * size, count * size)]
  transfers between devices with their start and end apart: 3 -> 0, of which waited for: 3 -> 0; matrix products, arithmetic and copies ran while one was open for 6% -> 0% of each run, Pallas kernels for 0% -> 0%
where the time goes in v2:
time: 77.3 us; the launch traced here: 77.1 us
  Pallas kernels  75.1 us (97%)
  local copies, waits for them, and re-layouts  1.35 us (2%)
    pallas_call x1, Pallas kernels, per_device(): pl.pallas_call(functools.partial(kernel, n, snake, k1, k0, size, LAGS), o...  69.8 us
    pallas_call x1, Pallas kernels, per_device(): pl.pallas_call(functools.partial(finish, k1, k0, size), out_shape=(jax.Sh...  5.31 us

profile of v2, /device:TPU:1, one launch (start us, length us, event | category | flops | bytes accessed | tf_op | source)
XLA Modules:
  0.0 77.1 jit_solution(6596088523102421434)
XLA Ops:
  0.6 1.4 %copy.14.pat_couple = s32[6,4]{1,0:T(8,128)} copy(s32[6,4]{0,1:T(4,128)} %param.16) | data formatting | bytes 192 | tf_op args[7]
  2.0 69.8 %shard_map.128 = (bf16[128,384]{1,0:T(8,128)(2,1)}, bf16[128,384]{1,0:T(8,128)(2,1)}, f32[128,512]{1,0:T(8,128)}, bf16[3584,128]{1,0:T(8,128)(2,1)}, bf16[2304,1...) custom-call(bf16[128,2048]{1,0:T(8,128)(2,1)} %anc.1, bf16[128,768]{1,0:T(8,128)(2,1)} %l_one.1, s32[1,6]{1,0:T(1,128)} %pat_one.1, ...), custom_call_target="tpu_custom_call" | custom-call | tf_op jit(solution)/shard_map/pallas_call | solution.py:316
  71.8 5.3 %shard_map.129 = (bf16[128,768]{1,0:T(8,128)(2,1)}, f32[768,768]{1,0:T(8,128)}, bf16[128,512]{1,0:T(8,128)(2,1)}, f32[768,512]{1,0:T(8,128)}, f32[512,512]{1,0:T(8,128)}) custom-call(bf16[128,384]{1,0:T(8,128)(2,1)} %get-tuple-element.11.x0, bf16[128,384]{1,0:T(8,128)(2,1)} %get-tuple-element.12.x1, f32[128,512]{1,0:T(8,128)} %get-tuple-element.13.x2, ...), custom_call_target="tpu_custom_call" | custom-call | tf_op jit(solution)/shard_map/pallas_call | solution.py:341
